TPU v7x, 512 devices: a whole 4x4x16 slice. The times are simulated.
512 devices in a mesh: chan: 64 (over z, y), blk: 8 (over x, core).
Axes of the slice: x: 4, y: 4, z: 16, core: 2. Of those that a mesh axis runs over, the one named last changes fastest.
Arguments:
- amps_pp: bfloat16 [64, 3584, 512], P('chan', 'blk'), may hold values from -6 to 6
- source_pp: bfloat16 [64, 3584, 512], P('chan', 'blk'), may hold values from -6 to 6
- cycle_interaction: bfloat16 [64, 3584, 3584], P('chan', 'blk'), may hold values from -1 to 1, as said below
- to_ph_rows: int32 [64, 3584, 2], P('chan', 'blk'), may hold values from 0 to 447
- to_ph_coef: int32 [64, 3584, 2], P('chan', 'blk'), may hold values from 0 to 255
- to_pp_rows: int32 [64, 3584, 2], P('chan', 'blk'), may hold values from 0 to 447
- to_pp_coef: int32 [64, 3584, 2], P('chan', 'blk'), may hold values from 0 to 255
- sixj: bfloat16 [256], replicated, may hold values from -1 to 1
- pp_sizes: int32 [64], replicated, may hold values from 1 to 3584, 76458 in all
- ph_sizes: int32 [64], replicated, may hold values from 1 to 3584, 76458 in all
- particle_energy: float32 [64, 3584], P('chan', 'blk'), may hold values from 1 to 4
- hole_energy: float32 [64, 512], P('chan'), may hold values from -3 to -0.5
Outputs:
- new_amps: bfloat16 [64, 3584, 512], P('chan', 'blk')
Inputs may be any that keep to these rules, and one draw needn't show every extreme that they name: `to_ph_rows`: row numbers within one device's block of 448 rows. `to_pp_rows`: row numbers within one device's block of 448 rows. `cycle_interaction`: each channel's matrix is symmetric.
All inputs are finite; a program needn't handle non-finite values.
Results may differ from a plain program's by a relative error of at most 0.0095.
Values may be sent and summed in bfloat16 or wider, within the bound.
A program may use at most 64 MiB of HBM per device.

v0:
```python
import jax
import jax.numpy as jnp
from jax import lax
from jax.sharding import PartitionSpec as P


def lookup(sixj, table):
    flat = table.reshape(-1)
    onehot = (flat[:, None] == jnp.arange(sixj.shape[0], dtype=jnp.int32)[None, :]).astype(
        jnp.float32
    )
    values = jnp.dot(onehot, sixj.astype(jnp.float32), precision=lax.Precision.HIGHEST)
    return values.reshape(table.shape)


def combine(rows, index, coef):
    first = jnp.take(rows, index[:, 0], axis=0).astype(jnp.float32)
    second = jnp.take(rows, index[:, 1], axis=0).astype(jnp.float32)
    return (first * coef[:, 0:1] + second * coef[:, 1:2]).astype(jnp.bfloat16)


def on_device(
    amps_pp,
    source_pp,
    cycle_interaction,
    to_ph_rows,
    to_ph_coef,
    to_pp_rows,
    to_pp_coef,
    sixj,
    pp_sizes,
    ph_sizes,
    particle_energy,
    hole_energy,
):
    local_rows = amps_pp.shape[1]
    channel = lax.axis_index("chan")
    block = lax.axis_index("blk")
    row_ids = block * local_rows + jnp.arange(local_rows, dtype=jnp.int32)
    coef_ph = lookup(sixj, to_ph_coef[0])
    slots = combine(amps_pp[0], to_ph_rows[0], coef_ph)
    arrived = lax.all_to_all(slots, "chan", split_axis=0, concat_axis=0, tiled=True)
    live_ph = row_ids < ph_sizes[channel]
    amps_ph = jnp.where(live_ph[:, None], arrived, jnp.zeros_like(arrived))
    inter_rows = cycle_interaction[0]
    cycle = lax.psum_scatter(
        lax.dot_general(
            inter_rows, amps_ph, (((0,), (0,)), ((), ())), preferred_element_type=jnp.float32
        ).astype(jnp.bfloat16),
        "blk",
        scatter_dimension=0,
        tiled=True,
    ).astype(jnp.float32)
    coef_pp = lookup(sixj, to_pp_coef[0])
    slots_back = combine(cycle, to_pp_rows[0], coef_pp)
    back = lax.all_to_all(slots_back, "chan", split_axis=0, concat_axis=0, tiled=True)
    denom = particle_energy[0][:, None] - hole_energy[0][None, :]
    value = (source_pp[0].astype(jnp.float32) + back.astype(jnp.float32)) / denom
    live_pp = row_ids < pp_sizes[channel]
    value = jnp.where(live_pp[:, None], value, jnp.zeros_like(value))
    return value.astype(jnp.bfloat16)[None]


def solution(mesh):
    in_specs = (
        P("chan", "blk", None),
        P("chan", "blk", None),
        P("chan", "blk", None),
        P("chan", "blk", None),
        P("chan", "blk", None),
        P("chan", "blk", None),
        P("chan", "blk", None),
        P(),
        P(),
        P(),
        P("chan", "blk"),
        P("chan", None),
    )
    out_specs = P("chan", "blk", None)
    return jax.shard_map(
        on_device, mesh=mesh, in_specs=in_specs, out_specs=out_specs, check_vma=False
    )
```

profile of v0, /device:TPU:6, one launch (start us, length us, event | category | flops | bytes accessed | tf_op | source)
XLA Modules:
  0.0 194.2 jit_solution(11184208750327668325)
XLA Ops:
  6.5 0.0 copy-start
  6.5 0.9 fusion.7
  7.5 0.0 copy-start.6
  7.5 0.0 copy-start.1
  7.5 3.8 %gather_fusion = bf16[448,512]{1,0:T(8,128)(2,1)} fusion(bf16[448,512]{1,0:T(8,128)(2,1)} %bitcast.20, s32[1024]{0:T(1024)S(1)} %pad_clamp_fusion.3), kind=kCustom, calls=%fused_computation.clone | custom fusion | bytes 919296 | tf_op jit(solution)/shard_map/jit(_take)/gather | solution.py:17
  11.2 3.7 %gather_fusion.1 = bf16[448,512]{1,0:T(8,128)(2,1)} fusion(bf16[448,512]{1,0:T(8,128)(2,1)} %bitcast.21, s32[1024]{0:T(1024)S(1)} %pad_clamp_fusion.2), kind=kCustom, calls=%fused_computation.2.clone | custom fusion | bytes 919296 | tf_op jit(solution)/shard_map/jit(_take)/gather | solution.py:18
  14.9 0.0 copy-done.6
  15.0 0.0 copy-done.1
  15.0 0.1 copy.23
  15.1 0.2 eq.30
  15.3 0.3 convolution_reduce_fusion.1
  15.6 0.2 reshape.107
  15.8 0.3 slice_reduce_fusion.3
  16.1 2.2 %add_convert_fusion = bf16[448,512]{1,0:T(8,128)(2,1)} fusion(bf16[448,512]{1,0:T(8,128)(2,1)} %gather_fusion.1, bf16[448,512]{1,0:T(8,128)(2,1)} %gather_fusion, f32[448]{0:T(512)S(1)} %get-tuple-element.10, f32[448]{0:T(512)S(1)} %get-tuple-element.9, pred[448]{0:T(512)(128)(4,1)S(1)} %get-tuple-element.15, pred[448]{0:T(512)(128)(4,1)S(1)} %get-tuple-element.16), kind=kLoop, calls=%fused_computation.15 | loop fusion | flops 1835008 | bytes 1380736 | tf_op jit(solution)/shard_map/convert_element_type | solution.py:19
  18.3 2.0 %all_to_all.12 = bf16[64,7,512]{2,1,0:T(8,128)(2,1)} reshape(bf16[448,512]{1,0:T(8,128)(2,1)} %add_convert_fusion) | data formatting | bytes 917504 | tf_op jit(solution)/shard_map/all_to_all | solution.py:42
  20.3 19.0 %all-to-all-start = ((bf16[64,7,512]{2,1,0:T(8,128)(2,1)}), bf16[64,7,512]{2,1,0:T(8,128)(2,1)}, u32[]{:S(2)}, u32[]{:S(2)}) async-start(bf16[64,7,512]{2,1,0:T(8,128)(2,1)} %all_to_all.12), calls=%async_computation | async-start | bytes 1048576 | tf_op jit(solution)/shard_map/all_to_all | solution.py:42
  39.3 0.0 reduce-scatter.4.cloned.1.call-start
  39.3 0.0 copy-done.7
  39.4 0.6 dynamic_slice.7
  39.9 0.7 add_compare_fusion
  40.6 0.1 copy.22
  40.7 31.2 %all-to-all-done = bf16[64,7,512]{2,1,0:T(8,128)(2,1)} async-done(((bf16[64,7,512]{2,1,0:T(8,128)(2,1)}), bf16[64,7,512]{2,1,0:T(8,128)(2,1)}, u32[]{:S(2)}, u32[]{:S(2)}) %all-to-all-start) | async-done | bytes 458784 | tf_op jit(solution)/shard_map/all_to_all | solution.py:42
  72.0 2.0 %broadcast_select_fusion = bf16[64,7,512]{2,1,0:T(8,128)(2,1)} fusion(bf16[64,7,512]{2,1,0:T(8,128)(2,1)} %all-to-all-done, pred[64,7]{1,0:T(8,128)(4,1)S(1)} %copy.22), kind=kLoop, calls=%fused_computation.17 | loop fusion | flops 229376 | bytes 917952 | tf_op jit(solution)/shard_map/jit(_where)/select_n | solution.py:44
  73.9 2.0 %select_n.31 = bf16[448,512]{1,0:T(8,128)(2,1)} reshape(bf16[64,7,512]{2,1,0:T(8,128)(2,1)} %broadcast_select_fusion) | data formatting | bytes 917504 | tf_op jit(solution)/shard_map/jit(_where)/select_n | solution.py:44
  75.9 0.0 copy-done
  75.9 5.0 %fusion = bf16[3584,512]{0,1:T(8,128)(2,1)} fusion(bf16[448,512]{1,0:T(8,128)(2,1)} %select_n.31, bf16[1,448,3584]{2,1,0:T(8,128)(2,1)S(1)} %copy-done), kind=kOutput, calls=%fused_computation.5 | convolution fusion | flops 1646002176 | bytes 7340032 | tf_op jit(solution)/shard_map/dot_general | solution.py:47
  80.8 5.9 %copy.26 = bf16[3584,512]{1,0:T(8,128)(2,1)} copy(bf16[3584,512]{0,1:T(8,128)(2,1)} %fusion) | data formatting | bytes 7340032
  86.8 0.0 reduce-scatter.4.cloned.1.call-update
  86.8 0.7 copy-done.2
  87.5 0.1 copy.25
  87.6 0.2 eq.34
  87.8 0.3 convolution_reduce_fusion
  88.1 0.2 reshape.108
  88.3 0.0 copy-done.3
  88.4 0.3 slice_reduce_fusion.1
  88.7 30.8 %reduce-scatter.4.cloned.1.call-done = bf16[448,512]{1,0:T(8,128)(2,1)} async-done(((bf16[3584,512]{1,0:T(8,128)(2,1)}), bf16[448,512]{1,0:T(8,128)(2,1)}) %reduce-scatter.4.cloned.1.call-update) | async-done | bytes 458768 | tf_op jit(solution)/shard_map/reduce_scatter | solution.py:46
  119.5 2.1 %convert_element_type.52 = f32[448,512]{1,0:T(8,128)} convert(bf16[448,512]{1,0:T(8,128)(2,1)} %reduce-scatter.4.cloned.1.call-done) | non-fusion elementwise | flops 229376 | bytes 1376256 | tf_op jit(solution)/shard_map/convert_element_type | solution.py:53
  121.5 3.9 %gather_fusion.2 = f32[448,512]{1,0:T(8,128)} fusion(f32[448,512]{1,0:T(8,128)} %convert_element_type.52, s32[1024]{0:T(1024)S(1)} %pad_clamp_fusion.1), kind=kCustom, calls=%fused_computation.1.clone | custom fusion | bytes 1836800 | tf_op jit(solution)/shard_map/jit(_take)/gather | solution.py:17
  125.4 3.9 %gather_fusion.3 = f32[448,512]{1,0:T(8,128)} fusion(f32[448,512]{1,0:T(8,128)} %convert_element_type.52, s32[1024]{0:T(1024)S(1)} %pad_clamp_fusion), kind=kCustom, calls=%fused_computation.3.clone | custom fusion | bytes 1836800 | tf_op jit(solution)/shard_map/jit(_take)/gather | solution.py:18
  129.3 2.6 %fusion.3 = bf16[448,512]{1,0:T(8,128)(2,1)} fusion(f32[448,512]{1,0:T(8,128)} %gather_fusion.3, f32[448,512]{1,0:T(8,128)} %gather_fusion.2, f32[448]{0:T(512)S(1)} %get-tuple-element.8, f32[448]{0:T(512)S(1)} %get-tuple-element.6, pred[448]{0:T(512)(128)(4,1)S(1)} %get-tuple-element.17, pred[448]{0:T(512)(128)(4,1)S(1)} %get-tuple-element.18), kind=kLoop, calls=%fused_computation.11 | loop fusion | flops 1376256 | bytes 2298240 | tf_op jit(solution)/shard_map/convert_element_type | solution.py:19
  131.8 1.9 %all_to_all.14 = bf16[64,7,512]{2,1,0:T(8,128)(2,1)} reshape(bf16[448,512]{1,0:T(8,128)(2,1)} %fusion.3) | data formatting | bytes 917504 | tf_op jit(solution)/shard_map/all_to_all | solution.py:56
  133.8 15.8 %all-to-all-start.1 = ((bf16[64,7,512]{2,1,0:T(8,128)(2,1)}), bf16[64,7,512]{2,1,0:T(8,128)(2,1)}, u32[]{:S(2)}, u32[]{:S(2)}) async-start(bf16[64,7,512]{2,1,0:T(8,128)(2,1)} %all_to_all.14), calls=%async_computation.1 | async-start | bytes 1048576 | tf_op jit(solution)/shard_map/all_to_all | solution.py:56
  149.6 0.0 copy-done.8
  149.6 0.6 dynamic_slice.6
  150.2 0.7 add_compare_fusion.1
  150.9 32.0 %all-to-all-done.1 = bf16[64,7,512]{2,1,0:T(8,128)(2,1)} async-done(((bf16[64,7,512]{2,1,0:T(8,128)(2,1)}), bf16[64,7,512]{2,1,0:T(8,128)(2,1)}, u32[]{:S(2)}, u32[]{:S(2)}) %all-to-all-start.1) | async-done | bytes 458784 | tf_op jit(solution)/shard_map/all_to_all | solution.py:56
  182.9 2.1 %reshape.109 = f32[1,448,512]{2,1,0:T(8,128)} reshape(bf16[64,7,512]{2,1,0:T(8,128)(2,1)} %all-to-all-done.1) | data formatting | bytes 1376256 | tf_op jit(solution)/shard_map/convert_element_type | solution.py:58
  185.0 2.3 %select_convert_fusion = bf16[1,448,512]{2,1,0:T(8,128)(2,1)} fusion(f32[1,448,512]{2,1,0:T(8,128)} %reshape.109, bf16[1,448,512]{2,1,0:T(8,128)(2,1)} %param.17, f32[512]{0:T(512)S(1)} %bitcast.32, f32[448]{0:T(512)S(1)} %bitcast.33, pred[448]{0:T(512)(128)(4,1)S(1)} %add_compare_fusion.1), kind=kLoop, calls=%fused_computation.13 | loop fusion | flops 1376256 | bytes 1839296 | tf_op jit(solution)/shard_map/convert_element_type | solution.py:61
  (20 shorter events, 0.1 us)
Async XLA Ops:
  6.5 69.4 %copy-start = (bf16[1,448,3584]{2,1,0:T(8,128)(2,1)S(1)}, bf16[1,448,3584]{2,1,0:T(8,128)(2,1)}, u32[]{:S(2)}) copy-start(bf16[1,448,3584]{2,1,0:T(8,128)(2,1)} %param.18) | copy-start | bytes 9633796
  7.5 7.5 %copy-start.6 = (bf16[256]{0:T(256)(128)(2,1)S(1)}, bf16[256]{0:T(256)(128)(2,1)}, u32[]{:S(2)}) copy-start(bf16[256]{0:T(256)(128)(2,1)} %param.23) | copy-start | bytes 1540
  7.5 7.5 %copy-start.1 = (s32[1,448,2]{1,2,0:T(2,128)S(1)}, s32[1,448,2]{1,2,0:T(2,128)}, u32[]{:S(2)}) copy-start(s32[1,448,2]{1,2,0:T(2,128)} %param.20) | copy-start | bytes 10756
  11.2 28.1 %copy-start.7 = (s32[64]{0:T(128)S(1)}, s32[64]{0:T(128)}, u32[]{:S(2)}) copy-start(s32[64]{0:T(128)} %param.25) | copy-start | bytes 772
  20.3 51.7 %all-to-all-start = ((bf16[64,7,512]{2,1,0:T(8,128)(2,1)}), bf16[64,7,512]{2,1,0:T(8,128)(2,1)}, u32[]{:S(2)}, u32[]{:S(2)}) async-start(bf16[64,7,512]{2,1,0:T(8,128)(2,1)} %all_to_all.12), calls=%async_computation | async-start | bytes 1048576 | tf_op jit(solution)/shard_map/all_to_all | solution.py:42
  39.3 80.2 %reduce-scatter.4.cloned.1.call-start = ((), (), s32[]{:S(2)}) async-start(), calls=%async_computation.3 | async-start | bytes 4128768 | tf_op jit(solution)/shard_map/reduce_scatter | solution.py:46
  86.8 0.7 copy-start.2
  86.8 1.5 copy-start.3
  129.3 20.4 %copy-start.8 = (s32[64]{0:T(128)S(1)}, s32[64]{0:T(128)}, u32[]{:S(2)}) copy-start(s32[64]{0:T(128)} %param.24) | copy-start | bytes 772
  129.3 55.8 %copy-start.4 = (f32[1,512]{1,0:T(1,128)S(1)}, f32[1,512]{1,0:T(1,128)}, u32[]{:S(2)}) copy-start(f32[1,512]{1,0:T(1,128)} %param.27) | copy-start | bytes 6148
  129.3 55.8 %copy-start.5 = (f32[1,448]{1,0:T(1,128)S(1)}, f32[1,448]{1,0:T(1,128)}, u32[]{:S(2)}) copy-start(f32[1,448]{1,0:T(1,128)} %param.26) | copy-start | bytes 5380
  133.8 49.1 %all-to-all-start.1 = ((bf16[64,7,512]{2,1,0:T(8,128)(2,1)}), bf16[64,7,512]{2,1,0:T(8,128)(2,1)}, u32[]{:S(2)}, u32[]{:S(2)}) async-start(bf16[64,7,512]{2,1,0:T(8,128)(2,1)} %all_to_all.14), calls=%async_computation.1 | async-start | bytes 1048576 | tf_op jit(solution)/shard_map/all_to_all | solution.py:56
Sparse Core Ops, SparseCore 0:
  86.9 32.5 reduce-scatter.3
where the time goes:
time: 196 us; the launch traced here: 194 us
  waiting for transfers between devices  94.1 us (48%)
  starting transfers between devices  34.9 us (18%)
  local copies, waits for them, and re-layouts  33.5 us (17%)
  between operations  13.6 us (7%)
  other arithmetic  12.5 us (6%)
  matrix products  5.62 us (3%)
    all_to_all x1, waiting for transfers between devices, on_device(): lax.all_to_all(slots_back, 'chan', split_axis=0, concat_axis=0, tiled=True)  32 us
    all_to_all x1, waiting for transfers between devices, on_device(): lax.all_to_all(slots, 'chan', split_axis=0, concat_axis=0, tiled=True)  31.2 us
    reduce_scatter x1, waiting for transfers between devices, on_device(): lax.psum_scatter(lax.dot_general(inter_rows, amps_ph, (((0,), (0,)), ((),...  30.8 us
    all_to_all x1, starting transfers between devices, on_device(): lax.all_to_all(slots, 'chan', split_axis=0, concat_axis=0, tiled=True)  19 us
    all_to_all x1, starting transfers between devices, on_device(): lax.all_to_all(slots_back, 'chan', split_axis=0, concat_axis=0, tiled=True)  15.8 us
    gather x2, local copies, waits for them, and re-layouts, combine(): first = jnp.take(rows, index[:, 0], axis=0).astype(jnp.float32)  7.61 us
    gather x2, local copies, waits for them, and re-layouts, combine(): second = jnp.take(rows, index[:, 1], axis=0).astype(jnp.float32)  7.58 us
    unnamed x22, local copies, waits for them, and re-layouts  6.89 us
  transfers between devices with their start and end apart: 3, of which 3 were waited for; matrix products, arithmetic and copies ran while one was open for 2% of the time, Pallas kernels for 0%

commit v1 on v0

v1 whole, which is shorter than its diff:
```python
import functools

import jax
import jax.numpy as jnp
from jax import lax
from jax.experimental import pallas as pl
from jax.experimental.pallas import tpu as pltpu
from jax.sharding import PartitionSpec as P

MESH = pl.DeviceIdType.MESH
BF = jnp.bfloat16
F32 = jnp.float32
I32 = jnp.int32
NZ, NY, NX = 16, 4, 4
SLOT = 7
U = NY * SLOT
ROWS = NZ * U
STACK = 4 * U
FWD = (0, 32, 64, 96, 112)
BWD = (0, 16, 48, 80, 112)
WIN = ((0, 32), (16, 64), (48, 96), (80, 112))


def iota(shape, dim):
    return lax.broadcasted_iota(I32, shape, dim)


def div7(v):
    return (v * 9363) >> 16


def div28(v):
    return (v * 2341) >> 16


def div112(v):
    return (v * 586) >> 16


def onehot_rows(column, width):
    hit = iota((column.shape[0], width), 1) == column
    return jnp.where(hit, 1.0, 0.0).astype(BF)


def natural_of(p):
    y = div112(p)
    r = p - y * 112
    z = div7(r)
    return (z * NY + y) * SLOT + (r - z * SLOT)


def dot(a, b):
    return jnp.dot(a, b, preferred_element_type=F32)


def dot_tn(a, b):
    return lax.dot_general(a, b, (((0,), (0,)), ((), ())), preferred_element_type=F32)


def weights(rows_ref, coef_ref, sixj, k, live):
    picked = (iota((256, ROWS), 0) == coef_ref[k : k + 1, :]).astype(F32).astype(BF)
    c = dot(sixj, picked)[0:1, :]
    if live is not None:
        c = jnp.where(live, c, 0.0)
    return jnp.where(iota((ROWS, ROWS), 0) == rows_ref[k : k + 1, :], c, 0.0)


def kernel(
    amps_ref,
    phr_ref,
    phc_ref,
    ppr_ref,
    ppc_ref,
    sixj_ref,
    pps_ref,
    phs_ref,
    pe_ref,
    he_ref,
    inter_hbm,
    src_hbm,
    out_ref,
    inter,
    src,
    ip,
    sf,
    rf,
    sy,
    g,
    ts,
    ry,
    sb,
    rb,
    mid0,
    mid1,
    mid2,
    mid3,
    back0,
    back1,
    back2,
    back3,
    fin0,
    fin1,
    fin2,
    fin3,
    pcol,
    load_sem,
    fs,
    fr,
    gs,
    gr,
    cs,
    cr,
    ys,
    yr,
    bs,
    br,
):
    chan = lax.axis_index("chan")
    blk = lax.axis_index("blk")
    z = chan // NY
    y = lax.rem(chan, NY)
    x = blk // 2
    core = lax.rem(blk, 2)
    other = 1 - core
    mid = (mid0, mid1, mid2, mid3)
    backs = (back0, back1, back2, back3)
    fin = (fin0, fin1, fin2, fin3)

    def z_target(i):
        j = 15 - i - 1
        m = j // 2 + 1
        d = m + lax.rem(j, 2) * (NZ - 2 * m)
        return lax.rem(z + d, NZ)

    def yx_target(i):
        return lax.rem(y + lax.rem(i, NY), NY), lax.rem(x + i // NY, NX)

    barrier = pltpu.get_barrier_semaphore()

    def greet_z(i, _):
        pl.semaphore_signal(
            barrier, inc=1, device_id=(z_target(i) * NY + y, blk), device_id_type=MESH
        )
        return 0

    def greet_yx(i, _):
        ty, tx = yx_target(i)
        pl.semaphore_signal(
            barrier, inc=1, device_id=(z * NY + ty, tx * 2 + core), device_id_type=MESH
        )
        return 0

    lax.fori_loop(0, 15, greet_z, 0)
    lax.fori_loop(1, 16, greet_yx, 0)
    pl.semaphore_signal(barrier, inc=1, device_id=(chan, x * 2 + other), device_id_type=MESH)

    load_inter = pltpu.make_async_copy(inter_hbm, inter, load_sem.at[0])
    load_src = pltpu.make_async_copy(src_hbm, src, load_sem.at[1])
    load_inter.start()
    load_src.start()

    sixj = jnp.broadcast_to(sixj_ref[...].astype(F32), (16, 256)).astype(BF)
    s16 = iota((16, 64), 0)
    sizes = phs_ref[...]
    parts = jnp.where(
        s16 == 0,
        sizes >> 6,
        jnp.where(s16 == 1, sizes & 63, jnp.where(s16 == 2, iota((16, 64), 1), 0)),
    )
    owner = div7(iota((64, ROWS), 1)) == iota((64, ROWS), 0)
    spread = dot(parts.astype(F32).astype(BF), jnp.where(owner, 1.0, 0.0).astype(BF))
    limit = spread[0:1, :] * 64.0 + spread[1:2, :]
    place = (
        (blk * ROWS + chan * SLOT).astype(F32)
        + iota((1, ROWS), 1).astype(F32)
        - 7.0 * spread[2:3, :]
    )
    live = place < limit
    amps = amps_ref[...]
    slots = (
        dot_tn(weights(phr_ref, phc_ref, sixj, 0, live).astype(BF), amps)
        + dot_tn(weights(phr_ref, phc_ref, sixj, 1, live).astype(BF), amps)
    ).astype(BF)
    for k in range(4):
        lo, hi = FWD[k], FWD[k + 1]
        n = hi - lo
        r = iota((NZ * n, 1), 0)
        zz = r >> (5 if n == 32 else 4)
        rho = lo + (r & (n - 1))
        q = div28(rho)
        col = (q - k) * ROWS + zz * U + (rho - q * U)
        if k < 3:
            sel = onehot_rows(col, 2 * ROWS)
            piece = dot(sel[:, :ROWS], slots[:, 128 * k : 128 * k + 128]) + dot(
                sel[:, ROWS:], slots[:, 128 * k + 128 : 128 * k + 256]
            )
        else:
            piece = dot(onehot_rows(col, ROWS), slots[:, 128 * k : 128 * k + 128])
        sf[:, lo:hi, :] = piece.astype(BF).reshape(NZ, n, 128)

    pl.semaphore_wait(barrier, 31)

    def send_z(source, dest, lo, hi, send, recv):
        span = pl.ds(lo, hi - lo)

        def go(i, _):
            tz = z_target(i)
            pltpu.make_async_remote_copy(
                src_ref=source.at[tz, span],
                dst_ref=dest.at[z, span],
                send_sem=send,
                recv_sem=recv,
                device_id=(tz * NY + y, blk),
                device_id_type=MESH,
            ).start()
            return 0

        lax.fori_loop(0, 15, go, 0)
        pltpu.make_async_copy(source.at[z, span], dest.at[z, span], recv).start()

    def arrived(ref, sem):
        pltpu.make_async_copy(ref, ref, sem).wait()

    for k in range(4):
        send_z(sf, rf, FWD[k], FWD[k + 1], fs, fr.at[k])

    mixed = (
        weights(ppr_ref, ppc_ref, sixj, 0, None) + weights(ppr_ref, ppc_ref, sixj, 1, None)
    ).astype(BF)
    order = jnp.where(
        iota((ROWS, ROWS), 0) == natural_of(iota((1, ROWS), 1)), 1.0, 0.0
    ).astype(BF)
    mixed = dot(mixed, order).astype(BF)
    p2 = iota((1, 2 * ROWS), 1)
    half = jnp.where(p2 >= ROWS, ROWS, 0)
    order2 = jnp.where(
        iota((2 * ROWS, 2 * ROWS), 0) == half + natural_of(p2 - half), 1.0, 0.0
    ).astype(BF)
    load_inter.wait()
    for i in range(NX):
        cols = pl.ds(2 * ROWS * i, 2 * ROWS)
        part = dot_tn(mixed, inter[:, cols]).astype(BF)
        ip[:, cols] = dot(part, order2).astype(BF)

    p = iota((ROWS, 1), 0)
    py = div112(p)
    pr = p - py * 112
    pz = div7(pr)
    pu = py * SLOT + pr - pz * SLOT
    nz = div28(p)
    nu = p - nz * U
    for q in range(4):
        w0, w1 = WIN[q]
        win = w1 - w0
        off = U * q - w0
        mid[q][...] = onehot_rows(pz * win + off + pu, NZ * win)
        fin[q][...] = onehot_rows(nz * win + off + nu, NZ * win)
    for k in range(4):
        lo, hi = BWD[k], BWD[k + 1]
        n = hi - lo
        r = iota((NZ * n, 1), 0)
        zz = r >> (5 if n == 32 else 4)
        rho = lo + (r & (n - 1))
        q = div28(rho)
        u = rho - q * U
        uy = div7(u)
        first = max(k - 1, 0)
        col = (q - first) * ROWS + uy * 112 + zz * SLOT + (u - uy * SLOT)
        backs[k][...] = onehot_rows(col, ROWS if k == 0 else 2 * ROWS)
    diag = iota((ROWS, ROWS), 0) == iota((ROWS, ROWS), 1)
    pcol[...] = jnp.broadcast_to(
        jnp.sum(jnp.where(diag, pe_ref[...], 0.0), axis=1, keepdims=True), (ROWS, 128)
    )
    load_src.wait()

    def stage_yx(q):
        w0, w1 = WIN[q]
        arrived(rf.at[:, pl.ds(FWD[q], FWD[q + 1] - FWD[q])], fr.at[q])
        rows = rf[:, w0:w1, :].reshape(NZ * (w1 - w0), 128)
        sy[q] = dot(mid[q][...], rows).astype(BF).reshape(NY, 112, 128)

        def go(i, _):
            ty, tx = yx_target(i)
            pltpu.make_async_remote_copy(
                src_ref=sy.at[q, ty],
                dst_ref=g.at[q, x, core, y],
                send_sem=gs.at[q],
                recv_sem=gr.at[q],
                device_id=(z * NY + ty, tx * 2 + core),
                device_id_type=MESH,
            ).start()
            return 0

        lax.fori_loop(1, 16, go, 0)
        pltpu.make_async_copy(sy.at[q, y], g.at[q, x, core, y], gr.at[q]).start()

    def to_other(q):
        return pltpu.make_async_remote_copy(
            src_ref=g.at[q, :, core],
            dst_ref=g.at[q, :, core],
            send_sem=cs.at[q],
            recv_sem=cr.at[q],
            device_id=(chan, x * 2 + other),
            device_id_type=MESH,
        )

    def stage_core(q):
        arrived(g.at[q, :, core], gr.at[q])
        to_other(q).start()

    def stage_mul(q):
        arrived(g.at[q, :, other], cr.at[q])
        total = dot(ip[...], g[q].reshape(8 * ROWS, 128))
        ts[q] = total.astype(BF).reshape(NY, 112, 128)

        def go(i, _):
            ty = lax.rem(y + i, NY)
            pltpu.make_async_remote_copy(
                src_ref=ts.at[q, ty],
                dst_ref=ry.at[q, y],
                send_sem=ys.at[q],
                recv_sem=yr.at[q],
                device_id=(z * NY + ty, blk),
                device_id_type=MESH,
            ).start()
            return 0

        lax.fori_loop(1, 4, go, 0)
        pltpu.make_async_copy(ts.at[q, y], ry.at[q, y], yr.at[q]).start()

    def stage_back(k):
        lo, hi = BWD[k], BWD[k + 1]
        arrived(ry.at[k], yr.at[k])
        if k == 0:
            piece = dot(backs[k][...], ry[k].reshape(ROWS, 128))
        else:
            piece = dot(backs[k][...], ry[k - 1 : k + 1].reshape(2 * ROWS, 128))
        sb[:, lo:hi, :] = piece.astype(BF).reshape(NZ, hi - lo, 128)
        send_z(sb, rb, lo, hi, bs, br.at[k])

    limit_pp = pps_ref[chan]
    keep = blk * ROWS + iota((ROWS, 128), 0) < limit_pp

    def finish(q):
        w0, w1 = WIN[q]
        cols = slice(128 * q, 128 * q + 128)
        back = dot(fin[q][...], rb[:, w0:w1, :].reshape(NZ * (w1 - w0), 128))
        value = (src[:, cols].astype(F32) + back) / (pcol[...] - he_ref[:, cols])
        out_ref[:, cols] = jnp.where(keep, value, 0.0).astype(BF)

    def back_in(k):
        arrived(rb.at[:, pl.ds(BWD[k], BWD[k + 1] - BWD[k])], br.at[k])

    stage_yx(0)
    stage_yx(1)
    stage_core(0)
    stage_mul(0)
    stage_yx(2)
    stage_core(1)
    stage_back(0)
    stage_mul(1)
    stage_yx(3)
    stage_core(2)
    stage_back(1)
    stage_mul(2)
    stage_core(3)
    stage_back(2)
    stage_mul(3)
    stage_back(3)
    back_in(0)
    back_in(1)
    finish(0)
    back_in(2)
    finish(1)
    back_in(3)
    finish(2)
    finish(3)

    most = sf.at[pl.ds(0, 15)]
    arrived(most, fs)
    arrived(most, bs)
    for q in range(4):
        arrived(most, gs.at[q])
        arrived(g.at[q, :, core], cs.at[q])
        arrived(sf.at[pl.ds(0, 3)], ys.at[q])


def on_device(
    amps_pp,
    source_pp,
    cycle_interaction,
    to_ph_rows,
    to_ph_coef,
    to_pp_rows,
    to_pp_coef,
    sixj,
    pp_sizes,
    ph_sizes,
    particle_energy,
    hole_energy,
):
    vmem = pl.BlockSpec(memory_space=pltpu.VMEM)
    anywhere = pl.BlockSpec(memory_space=pl.ANY)
    smem = pl.BlockSpec(memory_space=pltpu.SMEM)
    wins = [NZ * (b - a) for a, b in WIN]
    cuts = [NZ * (b - a) for a, b in zip(BWD[:-1], BWD[1:])]
    dma = pltpu.SemaphoreType.DMA
    out = pl.pallas_call(
        kernel,
        out_shape=jax.ShapeDtypeStruct((ROWS, 512), BF),
        in_specs=[vmem] * 6 + [smem] + [vmem] * 3 + [anywhere] * 2,
        out_specs=vmem,
        scratch_shapes=[
            pltpu.VMEM((ROWS, 8 * ROWS), BF),
            pltpu.VMEM((ROWS, 512), BF),
            pltpu.VMEM((ROWS, 8 * ROWS), BF),
            pltpu.VMEM((NZ, STACK, 128), BF),
            pltpu.VMEM((NZ, STACK, 128), BF),
            pltpu.VMEM((4, NY, 112, 128), BF),
            pltpu.VMEM((4, NX, 2, NY, 112, 128), BF),
            pltpu.VMEM((4, NY, 112, 128), BF),
            pltpu.VMEM((4, NY, 112, 128), BF),
            pltpu.VMEM((NZ, STACK, 128), BF),
            pltpu.VMEM((NZ, STACK, 128), BF),
            *[pltpu.VMEM((ROWS, w), BF) for w in wins],
            *[pltpu.VMEM((c, ROWS if i == 0 else 2 * ROWS), BF) for i, c in enumerate(cuts)],
            *[pltpu.VMEM((ROWS, w), BF) for w in wins],
            pltpu.VMEM((ROWS, 128), F32),
            dma((2,)),
            dma,
            dma((4,)),
            dma((4,)),
            dma((4,)),
            dma((4,)),
            dma((4,)),
            dma((4,)),
            dma((4,)),
            dma,
            dma((4,)),
        ],
        compiler_params=pltpu.CompilerParams(
            collective_id=0, has_side_effects=True, vmem_limit_bytes=48 << 20
        ),
        name="cycle",
    )(
        amps_pp[0],
        to_ph_rows[0].T,
        to_ph_coef[0].T,
        to_pp_rows[0].T,
        to_pp_coef[0].T,
        sixj.reshape(1, 256),
        pp_sizes,
        ph_sizes.reshape(1, 64),
        particle_energy,
        hole_energy,
        cycle_interaction[0],
        source_pp[0],
    )
    return out[None]


def solution(mesh):
    in_specs = (
        P("chan", "blk", None),
        P("chan", "blk", None),
        P("chan", "blk", None),
        P("chan", "blk", None),
        P("chan", "blk", None),
        P("chan", "blk", None),
        P("chan", "blk", None),
        P(),
        P(),
        P(),
        P("chan", "blk"),
        P("chan", None),
    )
    out_specs = P("chan", "blk", None)
    return jax.shard_map(
        on_device, mesh=mesh, in_specs=in_specs, out_specs=out_specs, check_vma=False
    )
```

time: 196 us -> 88.4 us (0.45)
  waiting for transfers between devices: 94.1 us -> 0 us
  Pallas kernels: 0 us -> 77.1 us
  starting transfers between devices: 34.9 us -> 0 us
  local copies, waits for them, and re-layouts: 33.5 us -> 10.8 us
  between operations: 13.6 us -> 0.02 us
  other arithmetic: 12.5 us -> 0 us
  matrix products: 5.62 us -> 0 us
    pallas_call x0 -> x1, Pallas kernels: none -> 77.1 us  [on_device(): pl.pallas_call(kernel, out_shape=jax.ShapeDtypeStruct((ROWS, 512), BF), i...]
    all_to_all x2 -> x0, waiting for transfers between devices: 63.3 us -> none  [the longest x1 32 us: on_device(): lax.all_to_all(slots_back, 'chan', split_axis=0, concat_axis=0, tiled=True)]
    all_to_all x2 -> x0, starting transfers between devices: 34.8 us -> none  [the longest x1 19 us: on_device(): lax.all_to_all(slots, 'chan', split_axis=0, concat_axis=0, tiled=True)]
    reduce_scatter x1 -> x0, waiting for transfers between devices: 30.8 us -> none  [on_device(): lax.psum_scatter(lax.dot_general(inter_rows, amps_ph, (((0,), (0,)), ((),...]
    gather x4 -> x0, local copies, waits for them, and re-layouts: 15.2 us -> none  [the longest x2 7.61 us: combine(): first = jnp.take(rows, index[:, 0], axis=0).astype(jnp.float32)]
    convert_element_type x4 -> x0, other arithmetic: 9.18 us -> none  [the longest x2 4.81 us: combine(): return (first * coef[:, 0:1] + second * coef[:, 1:2]).astype(jnp.bfloat16)]
    dot_general x3 -> x0, matrix products: 5.62 us -> none  [the longest x1 4.96 us: on_device(): lax.dot_general(inter_rows, amps_ph, (((0,), (0,)), ((), ())), preferred_...]
    all_to_all x2 -> x0, local copies, waits for them, and re-layouts: 3.9 us -> none  [the longest x1 1.96 us: on_device(): lax.all_to_all(slots, 'chan', split_axis=0, concat_axis=0, tiled=True)]
  transfers between devices with their start and end apart: 3 -> 0, of which waited for: 3 -> 0; matrix products, arithmetic and copies ran while one was open for 2% -> 0% of each run, Pallas kernels for 0% -> 0%
where the time goes in v1:
time: 88.4 us; the launch traced here: 87.9 us
  Pallas kernels  77.1 us (87%)
  local copies, waits for them, and re-layouts  10.8 us (12%)
    pallas_call x1, Pallas kernels, on_device(): pl.pallas_call(kernel, out_shape=jax.ShapeDtypeStruct((ROWS, 512), BF), i...  77.1 us
    unnamed x23, local copies, waits for them, and re-layouts  10.1 us

profile of v1, /device:TPU:6, one launch (start us, length us, event | category | flops | bytes accessed | tf_op | source)
XLA Modules:
  0.0 87.9 jit_solution(1843023376463726881)
XLA Ops:
  0.0 0.7 reshape.6.sixj_ref
  0.7 0.0 copy-start
  0.7 1.9 %copy-done = bf16[1,448,3584]{2,1,0:T(8,128)(2,1)S(1)} copy-done((bf16[1,448,3584]{2,1,0:T(8,128)(2,1)S(1)}, bf16[1,448,3584]{2,1,0:T(8,128)(2,1)}, u32[]{:S(2)}) %copy-start) | copy-done | bytes 3211288
  2.6 0.0 copy-start.1
  2.6 1.0 %copy-done.1 = bf16[1,448,512]{2,1,0:T(8,128)(2,1)S(1)} copy-done((bf16[1,448,512]{2,1,0:T(8,128)(2,1)S(1)}, bf16[1,448,512]{2,1,0:T(8,128)(2,1)}, u32[]{:S(2)}) %copy-start.1) | copy-done | bytes 458776
  3.6 0.0 copy-start.2
  3.6 1.0 %copy-done.2 = bf16[1,448,512]{2,1,0:T(8,128)(2,1)S(1)} copy-done((bf16[1,448,512]{2,1,0:T(8,128)(2,1)S(1)}, bf16[1,448,512]{2,1,0:T(8,128)(2,1)}, u32[]{:S(2)}) %copy-start.2) | copy-done | bytes 458776
  4.6 0.0 copy-start.3
  4.6 0.7 copy-done.3
  5.3 0.0 copy-start.4
  5.3 0.7 copy-done.4
  6.0 0.0 copy-start.5
  6.0 0.7 copy-done.5
  6.7 0.0 copy-start.6
  6.7 0.7 copy-done.6
  7.4 0.0 copy-start.7
  7.4 0.7 copy-done.7
  8.0 0.0 copy-start.8
  8.0 0.7 copy-done.8
  8.7 0.0 copy-start.9
  8.7 0.7 copy-done.9
  9.4 0.0 copy-start.10
  9.4 0.7 copy-done.10
  10.0 77.1 %cycle.1 = bf16[448,512]{1,0:T(8,128)(2,1)S(1)} custom-call(bf16[448,512]{1,0:T(8,128)(2,1)S(1)} %bitcast.19, s32[2,448]{1,0:T(2,128)S(1)} %bitcast.21, s32[2,448]{1,0:T(2,128)S(1)} %bitcast.22, s32[2,448]{1,0:T(2,128)S(1)} %bitcast.23, s32[2,448]{1,0:T(2,128)S(1)} %bitcast.24, bf16[1,256]{1,0:T(2,128)(2,1)S(1)} %reshape.6.sixj_ref, s32[64]{0:T(128)S(1)} %copy-done.9, ...), custom_call_target="tpu_custom_call" | custom-call | tf_op jit(solution)/shard_map/cycle/pallas_call | solution.py:408
  87.2 0.8 copy.14
Async XLA Ops:
  0.7 1.9 %copy-start = (bf16[1,448,3584]{2,1,0:T(8,128)(2,1)S(1)}, bf16[1,448,3584]{2,1,0:T(8,128)(2,1)}, u32[]{:S(2)}) copy-start(bf16[1,448,3584]{2,1,0:T(8,128)(2,1)} %param.14) | copy-start | bytes 9633796
  2.6 1.0 %copy-start.1 = (bf16[1,448,512]{2,1,0:T(8,128)(2,1)S(1)}, bf16[1,448,512]{2,1,0:T(8,128)(2,1)}, u32[]{:S(2)}) copy-start(bf16[1,448,512]{2,1,0:T(8,128)(2,1)} %param.12) | copy-start | bytes 1376260
  3.6 1.0 %copy-start.2 = (bf16[1,448,512]{2,1,0:T(8,128)(2,1)S(1)}, bf16[1,448,512]{2,1,0:T(8,128)(2,1)}, u32[]{:S(2)}) copy-start(bf16[1,448,512]{2,1,0:T(8,128)(2,1)} %param.13) | copy-start | bytes 1376260
  4.6 0.7 copy-start.3
  5.3 0.7 copy-start.4
  6.0 0.7 copy-start.5
  6.7 0.7 copy-start.6
  7.4 0.7 copy-start.7
  8.0 0.7 copy-start.8
  8.7 0.7 copy-start.9
  9.4 0.7 copy-start.10

commit v2 on v1

v2 whole, which is shorter than its diff:
```python
import functools
import types

import jax
import jax.numpy as jnp
import ml_dtypes
import numpy as np
from jax import lax
from jax.experimental import pallas as pl
from jax.experimental.pallas import tpu as pltpu
from jax.sharding import PartitionSpec as P

MESH = pl.DeviceIdType.MESH
BF = jnp.bfloat16
F32 = jnp.float32
I32 = jnp.int32
NZ, NY, NX = 16, 4, 4
SLOT = 7
U = NY * SLOT
ROWS = NZ * U
STACK = 4 * U
FWD = (0, 32, 64, 96, 112)
BWD = (0, 16, 48, 80, 112)
WIN = ((0, 32), (16, 64), (48, 96), (80, 112))


def iota(shape, dim):
    return lax.broadcasted_iota(I32, shape, dim)


def natural_of(p):
    y, rest = p // 112, p % 112
    return (rest // SLOT * NY + y) * SLOT + rest % SLOT


def ones_at(columns, width):
    return jnp.asarray((np.arange(width)[None, :] == columns[:, None]).astype(ml_dtypes.bfloat16))


@functools.cache
def shapes():
    return {name: (len(columns), width) for name, (columns, width) in columns_of().items()}


def columns_of():
    p = np.arange(ROWS)
    found = {
        "order": (np.argsort(natural_of(p)), ROWS),
        "order2": (np.concatenate([np.argsort(natural_of(p)) + h * ROWS for h in range(2)]), 2 * ROWS),
    }
    z, u = p // U, p % U
    moved = natural_of(p)
    for q, (w0, w1) in enumerate(WIN):
        column = z * (w1 - w0) + U * q - w0 + u
        found[f"mid{q}"] = (column[moved], NZ * (w1 - w0))
        found[f"fin{q}"] = (column, NZ * (w1 - w0))
    for k in range(4):
        for name, cuts, first in (("pack", FWD, k), ("back", BWD, max(k - 1, 0))):
            lo, hi = cuts[k], cuts[k + 1]
            i = np.arange(NZ * (hi - lo))
            zz, rho = i // (hi - lo), lo + i % (hi - lo)
            q, u = rho // U, rho % U
            row = zz * U + u if name == "pack" else u // SLOT * 112 + zz * SLOT + u % SLOT
            wide = hi - lo == 32
            found[f"{name}{k}"] = ((q - first) * ROWS + row, ROWS * (2 if wide else 1))
    return found


def selections():
    return {name: ones_at(*value) for name, value in columns_of().items()}


def dot(a, b):
    return jnp.dot(a, b, preferred_element_type=F32)


def dot_tn(a, b):
    return lax.dot_general(a, b, (((0,), (0,)), ((), ())), preferred_element_type=F32)


def weights(rows_ref, coef_ref, sixj, k, live):
    c = 0.0
    for h in range(2):
        hit = iota((128, ROWS), 0) + 128 * h == coef_ref[k : k + 1, :]
        c = c + dot(sixj[h], jnp.where(hit, 1.0, 0.0).astype(BF))[0:1, :]
    if live is not None:
        c = jnp.where(live, c, 0.0)
    return jnp.where(iota((ROWS, ROWS), 0) == rows_ref[k : k + 1, :], c, 0.0)


INPUTS = ["amps", "phr", "phc", "ppr", "ppc", "sixj", "pps", "phs", "pe", "he", "inter", "src"]
STAGES = ["sf", "rf", "sy", "g", "ts", "ry", "sb", "rb", "scale", "out"]
SEMS = ["load", "store", "fs", "fr", "gs", "gr", "cs", "cr", "ys", "yr", "bs", "br"]


def kernel(*refs):
    tables = list(shapes())
    names = (
        [n + "_hbm" for n in INPUTS + tables]
        + ["out_hbm"]
        + INPUTS
        + tables
        + ["ip"]
        + STAGES
        + [n + "_sem" for n in SEMS]
    )
    body(types.SimpleNamespace(**dict(zip(names, refs, strict=True))))


def body(r):
    amps_ref, phr_ref, phc_ref, ppr_ref, ppc_ref = r.amps, r.phr, r.phc, r.ppr, r.ppc
    sixj_ref, pps_ref, phs_ref, pe_ref, he_ref = r.sixj, r.pps, r.phs, r.pe, r.he
    inter, src, ip, scale = r.inter, r.src, r.ip, r.scale
    sf, rf, sy, g, ts, ry, sb, rb = r.sf, r.rf, r.sy, r.g, r.ts, r.ry, r.sb, r.rb
    out_ref, out_hbm, store_sem = r.out, r.out_hbm, r.store_sem
    fs, fr, gs, gr, cs, cr = r.fs_sem, r.fr_sem, r.gs_sem, r.gr_sem, r.cs_sem, r.cr_sem
    ys, yr, bs, br = r.ys_sem, r.yr_sem, r.bs_sem, r.br_sem
    chan = lax.axis_index("chan")
    blk = lax.axis_index("blk")
    z = chan // NY
    y = lax.rem(chan, NY)
    x = blk // 2
    core = lax.rem(blk, 2)
    other = 1 - core

    def z_target(i):
        j = 15 - i - 1
        m = j // 2 + 1
        d = m + lax.rem(j, 2) * (NZ - 2 * m)
        return lax.rem(z + d, NZ)

    def yx_target(i):
        return lax.rem(y + lax.rem(i, NY), NY), lax.rem(x + i // NY, NX)

    queue = (
        "phr",
        "phc",
        "sixj",
        "phs",
        "amps",
        "pack0",
        "ppr",
        "ppc",
        "order",
        "inter",
        "order2",
        "pack1",
        "mid0",
        "mid1",
        "pack2",
        "pack3",
        "mid2",
        "mid3",
        "back0",
        "back1",
        "back2",
        "back3",
        "pps",
        "pe",
        "he",
        "src",
        "fin0",
        "fin1",
        "fin2",
        "fin3",
    )

    def load(name):
        k = queue.index(name)
        return pltpu.make_async_copy(
            getattr(r, name + "_hbm"), getattr(r, name), r.load_sem.at[k]
        )

    def loaded(*names):
        for name in names:
            load(name).wait()

    def table(name):
        loaded(name)
        return getattr(r, name)[...]

    barrier = pltpu.get_barrier_semaphore()

    def greet_z(i, _):
        pl.semaphore_signal(
            barrier, inc=1, device_id=(z_target(i) * NY + y, blk), device_id_type=MESH
        )
        return 0

    def greet_yx(i, _):
        ty, tx = yx_target(i)
        pl.semaphore_signal(
            barrier, inc=1, device_id=(z * NY + ty, tx * 2 + core), device_id_type=MESH
        )
        return 0

    lax.fori_loop(0, 15, greet_z, 0)
    lax.fori_loop(1, 16, greet_yx, 0)
    pl.semaphore_signal(barrier, inc=1, device_id=(chan, x * 2 + other), device_id_type=MESH)
    for name in queue[:6]:
        load(name).start()


    loaded("phr", "phc", "sixj", "phs", "amps")
    for name in queue[6:11]:
        load(name).start()
    six32 = sixj_ref[...].astype(F32)
    sixj = [jnp.broadcast_to(six32[h : h + 1, :], (16, 128)).astype(BF) for h in range(2)]
    s16 = iota((16, 64), 0)
    sizes = phs_ref[...]
    parts = jnp.where(
        s16 == 0,
        sizes >> 6,
        jnp.where(s16 == 1, sizes & 63, jnp.where(s16 == 2, iota((16, 64), 1), 0)),
    )
    offset = iota((64, ROWS), 1) - SLOT * iota((64, ROWS), 0)
    owner = (offset >= 0) & (offset < SLOT)
    spread = dot(parts.astype(F32).astype(BF), jnp.where(owner, 1.0, 0.0).astype(BF))
    limit = spread[0:1, :] * 64.0 + spread[1:2, :]
    place = (
        (blk * ROWS + chan * SLOT).astype(F32)
        + iota((1, ROWS), 1).astype(F32)
        - 7.0 * spread[2:3, :]
    )
    live = place < limit
    amps = amps_ref[...]
    slots = (
        dot_tn(weights(phr_ref, phc_ref, sixj, 0, live).astype(BF), amps)
        + dot_tn(weights(phr_ref, phc_ref, sixj, 1, live).astype(BF), amps)
    ).astype(BF)

    def pack(k):
        lo, hi = FWD[k], FWD[k + 1]
        sel = table(f"pack{k}")
        piece = dot(sel[:, :ROWS], slots[:, 128 * k : 128 * k + 128])
        if k < 3:
            piece = piece + dot(sel[:, ROWS:], slots[:, 128 * k + 128 : 128 * k + 256])
        sf[:, lo:hi, :] = piece.astype(BF).reshape(NZ, hi - lo, 128)

    pack(0)
    pl.semaphore_wait(barrier, 31)

    def send_z(source, dest, lo, hi, send, recv):
        span = pl.ds(lo, hi - lo)

        def go(i, _):
            tz = z_target(i)
            pltpu.make_async_remote_copy(
                src_ref=source.at[tz, span],
                dst_ref=dest.at[z, span],
                send_sem=send,
                recv_sem=recv,
                device_id=(tz * NY + y, blk),
                device_id_type=MESH,
            ).start()
            return 0

        lax.fori_loop(0, 15, go, 0)
        pltpu.make_async_copy(source.at[z, span], dest.at[z, span], recv).start()

    def arrived(ref, sem):
        pltpu.make_async_copy(ref, ref, sem).wait()

    def out_z(k):
        send_z(sf, rf, FWD[k], FWD[k + 1], fs.at[k], fr.at[k])

    def left_z(k):
        arrived(sf.at[pl.ds(0, 15), pl.ds(FWD[k], FWD[k + 1] - FWD[k])], fs.at[k])

    out_z(0)
    for name in queue[11:]:
        load(name).start()

    loaded("ppr", "ppc")
    mixed = (
        weights(ppr_ref, ppc_ref, sixj, 0, None) + weights(ppr_ref, ppc_ref, sixj, 1, None)
    ).astype(BF)
    mixed = dot(mixed, table("order")).astype(BF)
    loaded("inter", "order2")

    def mix(i):
        cols = pl.ds(2 * ROWS * i, 2 * ROWS)
        part = dot_tn(mixed, inter[:, cols]).astype(BF)
        ip[:, cols] = dot(part, r.order2[...]).astype(BF)

    def make_scale():
        loaded("pps", "pe", "he", "src")
        diag = iota((ROWS, ROWS), 0) == iota((ROWS, ROWS), 1)
        pcol = jnp.sum(jnp.where(diag, pe_ref[...], 0.0), axis=1, keepdims=True)
        keep = blk * ROWS + iota((ROWS, 512), 0) < pps_ref[0, chan]
        scale[...] = jnp.where(keep, 1.0 / (pcol - he_ref[...]), 0.0)

    def stage_yx(q):
        w0, w1 = WIN[q]
        arrived(rf.at[:, pl.ds(FWD[q], FWD[q + 1] - FWD[q])], fr.at[q])
        rows = rf[:, w0:w1, :].reshape(NZ * (w1 - w0), 128)
        sy[q] = dot(table(f"mid{q}"), rows).astype(BF).reshape(NY, 112, 128)

        def go(i, _):
            ty, tx = yx_target(i)
            pltpu.make_async_remote_copy(
                src_ref=sy.at[q, ty],
                dst_ref=g.at[q, x, core, y],
                send_sem=gs.at[q],
                recv_sem=gr.at[q, x],
                device_id=(z * NY + ty, tx * 2 + core),
                device_id_type=MESH,
            ).start()
            return 0

        lax.fori_loop(1, 16, go, 0)
        pltpu.make_async_copy(sy.at[q, y], g.at[q, x, core, y], gr.at[q, x]).start()

    chips = [lax.rem(x + d, NX) for d in (0, 1, 3, 2)]

    def stage_core(q):
        for xs in chips:
            arrived(g.at[q, xs, core], gr.at[q, xs])
            pltpu.make_async_remote_copy(
                src_ref=g.at[q, xs, core],
                dst_ref=g.at[q, xs, core],
                send_sem=cs.at[q],
                recv_sem=cr.at[q, xs],
                device_id=(chan, x * 2 + other),
                device_id_type=MESH,
            ).start()

    def stage_mul(q):
        total = jnp.zeros((ROWS, 128), F32)
        for xs in chips:
            arrived(g.at[q, xs, other], cr.at[q, xs])
            cols = pl.ds(pl.multiple_of(xs * 2 * ROWS, 128), 2 * ROWS)
            total = total + dot(ip[:, cols], g[q, xs].reshape(2 * ROWS, 128))
        ts[q] = total.astype(BF).reshape(NY, 112, 128)

        def go(i, _):
            ty = lax.rem(y + i, NY)
            pltpu.make_async_remote_copy(
                src_ref=ts.at[q, ty],
                dst_ref=ry.at[q, y],
                send_sem=ys.at[q],
                recv_sem=yr.at[q],
                device_id=(z * NY + ty, blk),
                device_id_type=MESH,
            ).start()
            return 0

        lax.fori_loop(1, 4, go, 0)
        pltpu.make_async_copy(ts.at[q, y], ry.at[q, y], yr.at[q]).start()

    def stage_back(k):
        lo, hi = BWD[k], BWD[k + 1]
        arrived(ry.at[k], yr.at[k])
        sel = table(f"back{k}")
        if k == 0:
            piece = dot(sel, ry[k].reshape(ROWS, 128))
        else:
            piece = dot(sel, ry[k - 1 : k + 1].reshape(2 * ROWS, 128))
        sb[:, lo:hi, :] = piece.astype(BF).reshape(NZ, hi - lo, 128)
        send_z(sb, rb, lo, hi, bs, br.at[k])

    def store(q):
        cols = pl.ds(128 * q, 128)
        return pltpu.make_async_copy(
            out_ref.at[:, cols], out_hbm.at[:, cols], store_sem.at[q]
        )

    def finish(q):
        w0, w1 = WIN[q]
        cols = slice(128 * q, 128 * q + 128)
        back = dot(table(f"fin{q}"), rb[:, w0:w1, :].reshape(NZ * (w1 - w0), 128))
        value = (src[:, cols].astype(F32) + back) * scale[:, cols]
        out_ref[:, cols] = value.astype(BF)
        store(q).start()

    def back_in(k):
        arrived(rb.at[:, pl.ds(BWD[k], BWD[k + 1] - BWD[k])], br.at[k])

    mix(0)
    pack(1)
    mix(1)
    mix(2)
    left_z(0)
    out_z(1)
    pack(2)
    pack(3)
    stage_yx(0)
    mix(3)
    left_z(1)
    out_z(2)
    stage_yx(1)
    stage_core(0)
    stage_mul(0)
    left_z(2)
    out_z(3)
    stage_yx(2)
    stage_core(1)
    stage_back(0)
    stage_mul(1)
    stage_yx(3)
    stage_core(2)
    stage_back(1)
    stage_mul(2)
    stage_core(3)
    stage_back(2)
    stage_mul(3)
    make_scale()
    stage_back(3)
    back_in(0)
    back_in(1)
    finish(0)
    back_in(2)
    finish(1)
    back_in(3)
    finish(2)
    finish(3)
    for q in range(4):
        store(q).wait()
    most = sf.at[pl.ds(0, 15)]
    left_z(3)
    arrived(most, bs)
    for q in range(4):
        arrived(most, gs.at[q])
        arrived(g.at[q, :, core], cs.at[q])
        arrived(sf.at[pl.ds(0, 3)], ys.at[q])


def on_device(
    amps_pp,
    source_pp,
    cycle_interaction,
    to_ph_rows,
    to_ph_coef,
    to_pp_rows,
    to_pp_coef,
    sixj,
    pp_sizes,
    ph_sizes,
    particle_energy,
    hole_energy,
):
    hbm = pl.BlockSpec(memory_space=pltpu.HBM)
    dma = pltpu.SemaphoreType.DMA
    tables = selections()
    inputs = (
        amps_pp[0],
        to_ph_rows[0].T,
        to_ph_coef[0].T,
        to_pp_rows[0].T,
        to_pp_coef[0].T,
        sixj.reshape(2, 128),
        pp_sizes.reshape(1, 64),
        ph_sizes.reshape(1, 64),
        particle_energy,
        hole_energy,
        cycle_interaction[0],
        source_pp[0],
        *tables.values(),
    )
    held = [
        (pltpu.SMEM if name == "pps" else pltpu.VMEM)(value.shape, value.dtype)
        for name, value in zip(INPUTS + list(tables), inputs, strict=True)
    ]
    out = pl.pallas_call(
        kernel,
        out_shape=jax.ShapeDtypeStruct((ROWS, 512), BF),
        in_specs=[hbm] * len(inputs),
        out_specs=hbm,
        scratch_shapes=[
            *held,
            pltpu.VMEM((ROWS, 8 * ROWS), BF),
            pltpu.VMEM((NZ, STACK, 128), BF),
            pltpu.VMEM((NZ, STACK, 128), BF),
            pltpu.VMEM((4, NY, 112, 128), BF),
            pltpu.VMEM((4, NX, 2, NY, 112, 128), BF),
            pltpu.VMEM((4, NY, 112, 128), BF),
            pltpu.VMEM((4, NY, 112, 128), BF),
            pltpu.VMEM((NZ, STACK, 128), BF),
            pltpu.VMEM((NZ, STACK, 128), BF),
            pltpu.VMEM((ROWS, 512), F32),
            pltpu.VMEM((ROWS, 512), BF),
            dma((len(inputs),)),
            dma((4,)),
            dma((4,)),
            dma((4,)),
            dma((4,)),
            dma((4, NX)),
            dma((4,)),
            dma((4, NX)),
            dma((4,)),
            dma((4,)),
            dma,
            dma((4,)),
        ],
        compiler_params=pltpu.CompilerParams(
            collective_id=0, has_side_effects=True, vmem_limit_bytes=60 << 20
        ),
        name="cycle",
    )(*inputs)
    return out[None]


def solution(mesh):
    in_specs = (
        P("chan", "blk", None),
        P("chan", "blk", None),
        P("chan", "blk", None),
        P("chan", "blk", None),
        P("chan", "blk", None),
        P("chan", "blk", None),
        P("chan", "blk", None),
        P(),
        P(),
        P(),
        P("chan", "blk"),
        P("chan", None),
    )
    out_specs = P("chan", "blk", None)
    return jax.shard_map(
        on_device, mesh=mesh, in_specs=in_specs, out_specs=out_specs, check_vma=False
    )
```

time: 88.4 us -> 73.9 us (0.84)
  local copies, waits for them, and re-layouts: 10.8 us -> 1.82 us
  Pallas kernels: 77.1 us -> 70.9 us
    unnamed x23 -> x1, local copies, waits for them, and re-layouts: 10.1 us -> 1.82 us
    pallas_call x1, Pallas kernels: 77.1 us -> 70.9 us  [on_device(): pl.pallas_call(kernel, out_shape=jax.ShapeDtypeStruct((ROWS, 512), BF), i...]
where the time goes in v2:
time: 73.9 us; the launch traced here: 72.7 us
  Pallas kernels  70.9 us (96%)
  local copies, waits for them, and re-layouts  1.82 us (2%)
    pallas_call x1, Pallas kernels, on_device(): pl.pallas_call(kernel, out_shape=jax.ShapeDtypeStruct((ROWS, 512), BF), i...  70.9 us
    unnamed x1, local copies, waits for them, and re-layouts  1.82 us

profile of v2, /device:TPU:6, one launch (start us, length us, event | category | flops | bytes accessed | tf_op | source)
XLA Modules:
  0.0 72.7 jit_solution(14134741058139493496)
XLA Ops:
  0.0 70.9 %cycle.1 = bf16[448,512]{1,0:T(8,128)(2,1)} custom-call(bf16[448,512]{1,0:T(8,128)(2,1)} %bitcast.21, s32[2,448]{1,0:T(2,128)} %bitcast.23, s32[2,448]{1,0:T(2,128)} %bitcast.24, s32[2,448]{1,0:T(2,128)} %bitcast.25, s32[2,448]{1,0:T(2,128)} %bitcast.26, bf16[2,128]{1,0:T(2,128)(2,1)} %bitcast.27, s32[1,64]{1,0:T(1,128)} %bitcast.28, s32[1,64]{1,0:T(1,128)} %bitcast.29, ...), custom_call_target="tpu_custom_call" | custom-call | tf_op jit(solution)/shard_map/cycle/pallas_call | solution.py:464
  70.9 1.8 %copy.32 = bf16[1,448,512]{2,1,0:T(8,128)(2,1)} copy(bf16[1,448,512]{2,1,0:T(8,128)(2,1)} %bitcast.20) | data formatting | bytes 917504

commit v3 on v2

--- a/solution.py
+++ b/solution.py
@@ -308,7 +308,8 @@
             ).start()
             return 0
 
-        lax.fori_loop(1, 16, go, 0)
+        for dx in (2, 1, 3, 0):
+            lax.fori_loop(4 * dx + (dx == 0), 4 * dx + 4, go, 0)
         pltpu.make_async_copy(sy.at[q, y], g.at[q, x, core, y], gr.at[q, x]).start()
 
     chips = [lax.rem(x + d, NX) for d in (0, 1, 3, 2)]
@@ -334,7 +335,7 @@
         ts[q] = total.astype(BF).reshape(NY, 112, 128)
 
         def go(i, _):
-            ty = lax.rem(y + i, NY)
+            ty = lax.rem(y + lax.rem(i, 3) + 1, NY)
             pltpu.make_async_remote_copy(
                 src_ref=ts.at[q, ty],
                 dst_ref=ry.at[q, y],

time: 73.9 us -> 72.2 us (0.977)
  Pallas kernels: 70.9 us -> 69.8 us
    pallas_call x1, Pallas kernels: 70.9 us -> 69.8 us  [on_device(): pl.pallas_call(kernel, out_shape=jax.ShapeDtypeStruct((ROWS, 512), BF), i...]
where the time goes in v3:
time: 72.2 us; the launch traced here: 71.6 us
  Pallas kernels  69.8 us (97%)
  local copies, waits for them, and re-layouts  1.82 us (3%)
    pallas_call x1, Pallas kernels, on_device(): pl.pallas_call(kernel, out_shape=jax.ShapeDtypeStruct((ROWS, 512), BF), i...  69.8 us
    unnamed x1, local copies, waits for them, and re-layouts  1.82 us

profile of v3, /device:TPU:6, one launch (start us, length us, event | category | flops | bytes accessed | tf_op | source)
XLA Modules:
  0.0 71.6 jit_solution(9251647589564859137)
XLA Ops:
  0.0 69.8 %cycle.1 = bf16[448,512]{1,0:T(8,128)(2,1)} custom-call(bf16[448,512]{1,0:T(8,128)(2,1)} %bitcast.21, s32[2,448]{1,0:T(2,128)} %bitcast.23, s32[2,448]{1,0:T(2,128)} %bitcast.24, s32[2,448]{1,0:T(2,128)} %bitcast.25, s32[2,448]{1,0:T(2,128)} %bitcast.26, bf16[2,128]{1,0:T(2,128)(2,1)} %bitcast.27, s32[1,64]{1,0:T(1,128)} %bitcast.28, s32[1,64]{1,0:T(1,128)} %bitcast.29, ...), custom_call_target="tpu_custom_call" | custom-call | tf_op jit(solution)/shard_map/cycle/pallas_call | solution.py:465
  69.8 1.8 %copy.32 = bf16[1,448,512]{2,1,0:T(8,128)(2,1)} copy(bf16[1,448,512]{2,1,0:T(8,128)(2,1)} %bitcast.20) | data formatting | bytes 917504
